TPU v7x, 32 devices: a whole 2x2x4 slice. The times are simulated.
32 devices in a mesh: dp: 16 (over z, x, core), tensor: 2 (over y).
Axes of the slice: x: 2, y: 2, z: 4, core: 2. Of those that a mesh axis runs over, the one named last changes fastest.
Arguments:
- tokens: bfloat16 [64, 256, 768], P('dp'), may hold values from -6 to 6
- segment_ids: int32 [64, 256], P('dp'), may hold values from 0 to 3, never falling along the last dimension, each value on 1 to 128 neighbouring positions
- pass_embed: float32 [768], replicated, may hold values from -5 to 5
- w_qkv: bfloat16 [3, 768, 768], P(None, None, 'tensor'), may hold values from -0.21875 to 0.21875
- w_out: bfloat16 [768, 768], P('tensor'), may hold values from -0.75 to 0.75
- w_up: bfloat16 [768, 3072], P(None, 'tensor'), may hold values from -0.21875 to 0.21875
- w_down: bfloat16 [3072, 768], P('tensor'), may hold values from -0.109375 to 0.109375
- ln_gain: float32 [2, 768], replicated, may hold values from 0.5 to 1.5
- ln_bias: float32 [2, 768], replicated, may hold values from -1.5 to 1.5
- cotangent: bfloat16 [64, 512, 768], P('dp'), may hold values from -6 to 6
Outputs:
- out: bfloat16 [64, 512, 768], P('dp')
- grad_tokens: float32 [64, 256, 768], P('dp')
- grad_qkv: float32 [3, 768, 768], P(None, None, 'tensor')
- grad_out: float32 [768, 768], P('tensor')
- grad_up: float32 [768, 3072], P(None, 'tensor')
- grad_down: float32 [3072, 768], P('tensor')
- grad_gain: float32 [2, 768], replicated
- grad_bias: float32 [2, 768], replicated
- grad_pass: float32 [768], replicated
Inputs may be any that keep to these rules, and one draw needn't show every extreme that they name: `segment_ids`: along a row the ids never fall; a document holds at most 128 tokens and one in each row holds exactly 128.
All inputs are finite; a program needn't handle non-finite values.
Results may differ from a plain program's by a relative error of at most 0.019.
Values may be sent and summed in bfloat16 or wider, within the bound.
No kernel may reach another device: no remote copies, remote signals or barrier semaphores. Data moves between devices by JAX's collectives and lax.ppermute only.
A program may use at most 256 MiB of HBM per device.

v0:
```python
import jax
import jax.numpy as jnp
from jax import lax
from jax.sharding import PartitionSpec as P

HD = 64


eps_norm = 1e-05
neg_fill = -1000000000.0


def norm_parts(act_in, gain_row, bias_row):
    centred = act_in - jnp.mean(act_in, axis=-1, keepdims=True)
    inverse = lax.rsqrt(jnp.mean(centred * centred, axis=-1, keepdims=True) + eps_norm)
    normal = centred * inverse
    return (normal * gain_row + bias_row, normal, inverse)


def norm_back(grad_norm, normal, inverse, gain_row):
    scaled = grad_norm * gain_row
    centre = jnp.mean(scaled, axis=-1, keepdims=True)
    proj_mean = jnp.mean(scaled * normal, axis=-1, keepdims=True)
    return inverse * (scaled - centre - normal * proj_mean)


def build_mask(segments):
    place_ids = jnp.arange(segments.shape[1], dtype=jnp.int32)
    causal = (place_ids[:, None] >= place_ids[None, :])[None]
    return (segments[:, :, None] == segments[:, None, :]) & causal


def masked_scores(queries, key_heads, visible):
    scores = jnp.einsum(
        "rqhe,rkhe->rhqk", queries, key_heads, preferred_element_type=jnp.float32
    ) * HD ** (-0.5)
    return jnp.where(visible[:, None], scores, neg_fill)


def gelu_tanh(values):
    return jax.nn.gelu(values, approximate=True)


def forward_block(act_in, visible, weights):
    w_qkv, w_out, w_up, w_down, ln_gain, ln_bias = weights
    row_count, length, model_width = act_in.shape
    heads_here = w_qkv.shape[2] // HD
    normed_one, hat_one, inv_one = norm_parts(act_in, ln_gain[0], ln_bias[0])
    normed_low = normed_one.astype(jnp.bfloat16)
    projected = jnp.einsum(
        "rld,kde->krle", normed_low, w_qkv, preferred_element_type=jnp.float32
    ).astype(jnp.bfloat16)
    head_view = projected.reshape(3, row_count, length, heads_here, HD)
    scores = masked_scores(head_view[0], head_view[1], visible)
    top_score = jnp.max(scores, axis=-1, keepdims=True)
    exp_scores = jnp.exp(scores - top_score)
    total_mass = jnp.sum(exp_scores, axis=-1, keepdims=True)
    log_mass = top_score + jnp.log(total_mass)
    soft_low = (exp_scores / total_mass).astype(jnp.bfloat16)
    attended = jnp.einsum(
        "rhqk,rkhe->rqhe", soft_low, head_view[2], preferred_element_type=jnp.float32
    )
    attended = attended.reshape(row_count, length, heads_here * HD).astype(jnp.bfloat16)
    attn_term = jnp.einsum("rld,de->rle", attended, w_out, preferred_element_type=jnp.float32)
    after_attn = act_in + lax.psum(attn_term.astype(jnp.bfloat16), "tensor").astype(jnp.float32)
    normed_two, hat_two, inv_two = norm_parts(after_attn, ln_gain[1], ln_bias[1])
    second_low = normed_two.astype(jnp.bfloat16)
    pre_act = jnp.einsum("rld,df->rlf", second_low, w_up, preferred_element_type=jnp.float32)
    hidden = gelu_tanh(pre_act).astype(jnp.bfloat16)
    down_term = jnp.einsum("rlf,fd->rld", hidden, w_down, preferred_element_type=jnp.float32)
    result = after_attn + lax.psum(down_term.astype(jnp.bfloat16), "tensor").astype(jnp.float32)
    kept = (
        normed_low,
        hat_one,
        inv_one,
        head_view,
        log_mass,
        attended,
        second_low,
        hat_two,
        inv_two,
        pre_act,
        hidden,
    )
    return (result, kept)


def backward_block(grad_result, visible, kept, weights):
    w_qkv, w_out, w_up, w_down, ln_gain, ln_bias = weights
    (
        normed_low,
        hat_one,
        inv_one,
        head_view,
        log_mass,
        attended,
        second_low,
        hat_two,
        inv_two,
        pre_act,
        hidden,
    ) = kept
    row_count, length, model_width = grad_result.shape
    grad_low = grad_result.astype(jnp.bfloat16)
    grad_down = jnp.einsum("rlf,rld->fd", hidden, grad_low, preferred_element_type=jnp.float32)
    grad_hidden = jnp.einsum("rld,fd->rlf", grad_low, w_down, preferred_element_type=jnp.float32)
    gelu_pull = jax.vjp(gelu_tanh, pre_act)[1]
    grad_pre = gelu_pull(grad_hidden)[0].astype(jnp.bfloat16)
    grad_up = jnp.einsum("rld,rlf->df", second_low, grad_pre, preferred_element_type=jnp.float32)
    up_term = jnp.einsum("rlf,df->rld", grad_pre, w_up, preferred_element_type=jnp.float32)
    grad_second = lax.psum(up_term.astype(jnp.bfloat16), "tensor").astype(jnp.float32)
    grad_mid = grad_result + norm_back(grad_second, hat_two, inv_two, ln_gain[1])
    mid_low = grad_mid.astype(jnp.bfloat16)
    grad_wout = jnp.einsum("rld,rle->de", attended, mid_low, preferred_element_type=jnp.float32)
    grad_att = jnp.einsum("rle,de->rld", mid_low, w_out, preferred_element_type=jnp.float32)
    grad_att = grad_att.astype(jnp.bfloat16).reshape(row_count, length, -1, HD)
    scores = masked_scores(head_view[0], head_view[1], visible)
    soft = jnp.exp(scores - log_mass)
    soft_low = soft.astype(jnp.bfloat16)
    grad_value = jnp.einsum(
        "rhqk,rqhe->rkhe", soft_low, grad_att, preferred_element_type=jnp.float32
    )
    grad_soft = jnp.einsum(
        "rqhe,rkhe->rhqk", grad_att, head_view[2], preferred_element_type=jnp.float32
    )
    weighted = jnp.sum(grad_soft * soft, axis=-1, keepdims=True)
    grad_scores = (soft * (grad_soft - weighted)).astype(jnp.bfloat16)
    grad_query = jnp.einsum(
        "rhqk,rkhe->rqhe", grad_scores, head_view[1], preferred_element_type=jnp.float32
    ) * HD ** (-0.5)
    grad_key = jnp.einsum(
        "rhqk,rqhe->rkhe", grad_scores, head_view[0], preferred_element_type=jnp.float32
    ) * HD ** (-0.5)
    grad_proj = (
        jnp.stack([grad_query, grad_key, grad_value])
        .reshape(3, row_count, length, -1)
        .astype(jnp.bfloat16)
    )
    grad_wqkv = jnp.einsum(
        "rld,krle->kde", normed_low, grad_proj, preferred_element_type=jnp.float32
    )
    qkv_term = jnp.einsum("krle,kde->rld", grad_proj, w_qkv, preferred_element_type=jnp.float32)
    grad_first = lax.psum(qkv_term.astype(jnp.bfloat16), "tensor").astype(jnp.float32)
    grad_in = grad_mid + norm_back(grad_first, hat_one, inv_one, ln_gain[0])
    grad_gain = jnp.stack(
        [jnp.sum(grad_first * hat_one, axis=(0, 1)), jnp.sum(grad_second * hat_two, axis=(0, 1))]
    )
    grad_bias = jnp.stack([jnp.sum(grad_first, axis=(0, 1)), jnp.sum(grad_second, axis=(0, 1))])
    return ((grad_wqkv, grad_wout, grad_up, grad_down, grad_gain, grad_bias), grad_in)


def shards(
    tokens, segment_ids, pass_embed, w_qkv, w_out, w_up, w_down, ln_gain, ln_bias, cotangent
):
    weights = (w_qkv, w_out, w_up, w_down, ln_gain, ln_bias)
    act_in = tokens.astype(jnp.float32)
    row_count, seq_len, model_width = act_in.shape
    mask_one = build_mask(segment_ids)
    mask_two = build_mask(jnp.repeat(segment_ids, 2, axis=1))
    first_out, kept_one = forward_block(act_in, mask_one, weights)
    alternated = jnp.stack([act_in, first_out + pass_embed[None, None]], axis=2).reshape(
        row_count, 2 * seq_len, model_width
    )
    second_out, kept_two = forward_block(alternated, mask_two, weights)
    grads_two, grad_inter = backward_block(
        cotangent.astype(jnp.float32), mask_two, kept_two, weights
    )
    split_grad = grad_inter.reshape(row_count, seq_len, 2, model_width)
    grad_pass = jnp.sum(split_grad[:, :, 1], axis=(0, 1))
    qkv_two, wout_two, up_two, down_two, gain_two, bias_two = grads_two
    grads_one, grad_first_in = backward_block(split_grad[:, :, 1], mask_one, kept_one, weights)
    grad_tokens = grad_first_in + split_grad[:, :, 0]
    qkv_one, wout_one, up_one, down_one, gain_one, bias_one = grads_one
    merged = (
        qkv_one + qkv_two,
        wout_one + wout_two,
        up_one + up_two,
        down_one + down_two,
        gain_one + gain_two,
        bias_one + bias_two,
        grad_pass,
    )
    totals = lax.psum(
        (merged[0], merged[1], merged[2], merged[3], merged[4], merged[5], merged[6]), "dp"
    )
    out_low = second_out.astype(jnp.bfloat16)
    return (
        out_low,
        grad_tokens,
        totals[0],
        totals[1],
        totals[2],
        totals[3],
        totals[4],
        totals[5],
        totals[6],
    )


def solution(mesh):
    placed = (
        P("dp", None, None),
        P("dp", None),
        P(),
        P(None, None, "tensor"),
        P("tensor", None),
        P(None, "tensor"),
        P("tensor", None),
        P(),
        P(),
        P("dp", None, None),
    )
    return jax.shard_map(
        shards,
        mesh=mesh,
        in_specs=placed,
        out_specs=(
            P("dp", None, None),
            P("dp", None, None),
            P(None, None, "tensor"),
            P("tensor", None),
            P(None, "tensor"),
            P("tensor", None),
            P(),
            P(),
            P(),
        ),
        check_vma=False,
    )
```

profile of v0, /device:TPU:0, one launch (start us, length us, event | category | flops | bytes accessed | tf_op | source)
XLA Modules:
  0.0 1145.1 jit_solution(17350992254646015082)
XLA Ops:
  11.3 4.0 convert_bitcast_fusion.2
  19.3 2.6 copy.91
  31.8 54.1 %all-reduce.12.cloned.1.call-done = bf16[4,256,768]{2,1,0:T(8,128)(2,1)} async-done(((bf16[4,256,768]{2,1,0:T(8,128)(2,1)}), bf16[4,256,768]{2,1,0:T(8,128)(2,1)}) %all-reduce.12.cloned.1.call-update) | async-done | bytes 1572880 | tf_op jit(solution)/shard_map/psum | solution.py:65
  89.5 2.8 fusion.82
  92.4 2.7 copy-done.84
  95.1 4.8 fusion.98
  101.3 3.3 convert_bitcast_fusion
  104.7 46.9 %all-reduce.14.cloned.1.call-done = bf16[4,256,768]{2,1,0:T(8,128)(2,1)} async-done(((bf16[4,256,768]{2,1,0:T(8,128)(2,1)}), bf16[4,256,768]{2,1,0:T(8,128)(2,1)}) %all-reduce.14.cloned.1.call-update) | async-done | bytes 1572880 | tf_op jit(solution)/shard_map/psum | solution.py:71
  151.6 3.1 add_bitcast_fusion
  154.9 3.0 pad_maximum_fusion
  159.7 9.4 copy.96
  172.2 7.8 convert_bitcast_fusion.1
  180.4 10.8 fusion.142
  191.2 10.1 fusion
  201.4 10.7 fusion.94
  213.3 3.5 convolution_convert_fusion
  216.9 85.9 %all-reduce.16.cloned.1.call-done = bf16[4,512,768]{2,1,0:T(8,128)(2,1)} async-done(((bf16[4,512,768]{2,1,0:T(8,128)(2,1)}), bf16[4,512,768]{2,1,0:T(8,128)(2,1)}) %all-reduce.16.cloned.1.call-update) | async-done | bytes 3145744 | tf_op jit(solution)/shard_map/psum | solution.py:65
  302.8 5.0 fusion.138
  311.3 8.6 fusion.80
  319.9 13.3 %fusion.8 = bf16[4,512,1536]{2,1,0:T(8,128)(2,1)S(1)} fusion(f32[4,512,1536]{2,1,0:T(8,128)} %fusion.80, bf16[4,512,768]{2,1,0:T(8,128)(2,1)S(1)} %copy-done.32, bf16[1536,768]{1,0:T(8,128)(2,1)S(1)} %copy-done), kind=kOutput, calls=%fused_computation.16 | convolution fusion | flops 4894752768 | bytes 24379392 | tf_op jit(solution)/shard_map/rld,fd->rlf/dot_general | solution.py:106
  333.2 2.6 copy-done.29
  335.8 6.4 fusion.84
  342.3 85.8 %all-reduce.18.cloned.1.call-done = bf16[4,512,768]{2,1,0:T(8,128)(2,1)} async-done(((bf16[4,512,768]{2,1,0:T(8,128)(2,1)}), bf16[4,512,768]{2,1,0:T(8,128)(2,1)}) %all-reduce.18.cloned.1.call-update) | async-done | bytes 3145744 | tf_op jit(solution)/shard_map/psum | solution.py:111
  428.2 6.3 fusion.34
  434.5 4.8 fusion.25
  439.4 3.2 convolution_convert_fusion.1
  442.6 17.0 %multiply_reduce_fusion = (f32[4,6,512]{2,1,0:T(8,128)S(1)}, f32[4,6,512,512]{2,3,1,0:T(8,128)}) fusion(f32[4,6,512,512]{2,3,1,0:T(8,128)} %get-tuple-element.81, f32[4,6,512]{2,1,0:T(8,128)S(1)} %log_add_fusion, bf16[4,512,6,64]{1,3,2,0:T(8,128)(2,1)} %bitcast.186, bf16[4,512,6,64]{1,3,2,0:T(8,128)(2,1)} %bitcast.199), kind=kOutput, calls=%fused_computation.1 | convolution fusion | flops 824168448 | bytes 53575680 | tf_op jit(solution)/shard_map/rqhe,rkhe->rhqk/dot_general | solution.py:123
  459.6 17.3 %multiply_convert_fusion = bf16[4,6,512,512]{2,3,1,0:T(8,128)(2,1)S(1)} fusion(f32[4,6,512,512]{2,3,1,0:T(8,128)} %get-tuple-element.83, f32[4,6,512,512]{2,3,1,0:T(8,128)} %get-tuple-element.81, f32[4,6,512]{2,1,0:T(8,128)S(1)} %get-tuple-element.82, f32[4,6,512]{2,1,0:T(8,128)S(1)} %log_add_fusion), kind=kLoop, calls=%fused_computation | loop fusion | flops 25165824 | bytes 63012864 | tf_op jit(solution)/shard_map/convert_element_type | solution.py:127
  476.9 4.6 copy-done.8
  481.5 3.3 multiply_convert_fusion.5
  484.7 9.6 multiply_convert_fusion.4
  494.4 13.7 %fusion.101 = bf16[4,6,64,512]{3,2,1,0:T(8,128)(2,1)} fusion(bf16[4,512,6,64]{1,3,2,0:T(8,128)(2,1)} %bitcast.187, f32[4,6,512,512]{2,3,1,0:T(8,128)} %get-tuple-element.81, f32[4,6,512]{2,1,0:T(8,128)S(1)} %log_add_fusion), kind=kOutput, calls=%fused_computation.155 | convolution fusion | flops 818675712 | bytes 28360704 | tf_op jit(solution)/shard_map/rhqk,rqhe->rkhe/dot_general | solution.py:120
  508.1 2.6 copy.112
  510.7 2.7 copy.113
  513.3 2.6 copy.114
  515.9 8.9 bitcast_convert_fusion
  525.7 11.7 %fusion.87 = bf16[4,512,768]{2,1,0:T(8,128)(2,1)} fusion(bf16[1536,768]{1,0:T(8,128)(2,1)S(1)} %copy-done, f32[4,512,1536]{2,1,0:T(8,128)} %fusion.80), kind=kOutput, calls=%fused_computation.144 | convolution fusion | flops 4861722624 | bytes 18087936 | tf_op jit(solution)/shard_map/rlf,fd->rld/dot_general | solution.py:70
  537.4 73.4 %all-reduce.20.cloned.1.call-done = bf16[4,512,768]{2,1,0:T(8,128)(2,1)} async-done(((bf16[4,512,768]{2,1,0:T(8,128)(2,1)}), bf16[4,512,768]{2,1,0:T(8,128)(2,1)}) %all-reduce.20.cloned.1.call-update) | async-done | bytes 3145744 | tf_op jit(solution)/shard_map/psum | solution.py:143
  610.8 6.7 fusion.35
  617.6 7.0 fusion.21
  624.6 4.0 copy.115
  628.7 3.0 slice_reduce_fusion.4
  631.7 6.0 fusion.33
  637.7 5.5 fusion.121
  643.2 3.8 fusion.95
  647.1 12.6 %bitcast_add_fusion = f32[1536,768]{1,0:T(8,128)} fusion(f32[1536,768,1]{1,0,2:T(8,128)} %fusion.121, bf16[4,512,768]{2,1,0:T(8,128)(2,1)} %param.19, f32[4,512,1536]{2,1,0:T(8,128)} %fusion.80), kind=kOutput, calls=%fused_computation.82 | convolution fusion | flops 4861329408 | bytes 25165824 | tf_op jit(solution)/shard_map/rlf,rld->fd/dot_general | solution.py:105
  659.7 39.0 %all-reduce.22.cloned.1.call-done = bf16[4,256,768]{2,1,0:T(8,128)(2,1)} async-done(((bf16[4,256,768]{2,1,0:T(8,128)(2,1)}), bf16[4,256,768]{2,1,0:T(8,128)(2,1)}) %all-reduce.22.cloned.1.call-update) | async-done | bytes 1572880 | tf_op jit(solution)/shard_map/psum | solution.py:111
  698.7 3.5 fusion.61
  702.5 3.0 fusion.59
  710.4 7.2 multiply_reduce_fusion.1
  717.6 4.5 multiply_convert_fusion.2
  733.5 5.6 bitcast_convert_fusion.1
  739.7 6.1 fusion.134
  745.8 12.7 %bitcast_add_fusion.1 = f32[768,1536]{1,0:T(8,128)} fusion(f32[768,1536,1]{1,0,2:T(8,128)S(1)} %fusion.134, bf16[4,512,1536]{2,1,0:T(8,128)(2,1)} %copy-done.29, f32[4,512,768]{2,1,0:T(8,128)} %copy-done.1, f32[768]{0:T(1024)S(1)} %copy-done.57, f32[768]{0:T(1024)S(1)} %get-tuple-element.87, f32[4,512]{1,0:T(4,128)S(1)} %copy-done.49, ...), kind=kOutput, calls=%fused_computation.83 | convolution fusion | flops 4840882176 | bytes 22042624 | tf_op jit(solution)/shard_map/rld,rlf->df/dot_general | solution.py:109
  762.4 2.8 fusion.118
  766.1 7.1 fusion.48
  773.9 84.9 %all-reduce.26.cloned.1.call-done = (bf16[4,512,768]{2,1,0:T(8,128)(2,1)}, bf16[4,256,768]{2,1,0:T(8,128)(2,1)}) async-done(((bf16[4,512,768]{2,1,0:T(8,128)(2,1)}, bf16[4,256,768]{2,1,0:T(8,128)(2,1)}), (bf16[4,512,768]{2,1,0:T(8,128)(2,1)}, bf16[4,256,768]{2,1,0:T(8,128)(2,1)})) %all-reduce.26.cloned.1.call-update) | async-done | bytes 4718608 | tf_op jit(solution)/shard_map/psum | solution.py:71
  858.8 3.0 fusion.62
  861.8 64.2 %all-reduce = (f32[2,768]{1,0:T(2,128)}, f32[2,768]{1,0:T(2,128)}, f32[768]{0:T(1024)}) all-reduce(f32[2,768]{1,0:T(2,128)S(1)} %maximum_add_fusion, f32[2,768]{1,0:T(2,128)S(1)} %maximum_add_fusion.1, f32[768]{0:T(1024)S(1)} %get-tuple-element.67), channel_id=1, replica_groups=mesh['dp'=16,'tensor'=2] {'dp'}, use_global_device_ids=true, to_apply=%region_38.39 | all-reduce | flops 3840 | bytes 30720 | tf_op jit(solution)/shard_map/psum | solution.py:183
  926.0 6.3 add_convert_fusion
  933.8 2.7 fusion.54
  936.5 187.3 %all-reduce.24.cloned.1.call-done = (f32[3,768,384]{1,2,0:T(8,128)}, f32[384,768]{1,0:T(8,128)}, f32[768,1536]{1,0:T(8,128)}, f32[1536,768]{1,0:T(8,128)}) async-done(((f32[3,768,384]{1,2,0:T(8,128)}, f32[384,768]{1,0:T(8,128)}, f32[768,1536]{1,0:T(8,128)}, f32[1536,768]{1,0:T(8,128)}), (f32[3,768,384]{1,2,0:T(8,128)}, f32[384,768]{1,0:T(8,128)}, f32[768,1536]{1,0:T(8,128)}, ...) | async-done | bytes 14155792 | tf_op jit(solution)/shard_map/psum | solution.py:183
  1123.9 5.2 copy.131
  1130.1 5.5 copy.193
  (274 shorter events, 61.1 us)
Async XLA Ops:
  7.2 87.9 %copy-start = (bf16[1536,768]{1,0:T(8,128)(2,1)S(1)}, bf16[1536,768]{1,0:T(8,128)(2,1)}, u32[]{:S(2)}) copy-start(bf16[1536,768]{1,0:T(8,128)(2,1)} %param.16) | copy-start | bytes 7077892
  7.2 4.0 copy-start.74
  7.2 4.0 copy-start.73
  7.2 78.7 %all-reduce.12.cloned.1.call-start = ((), (), s32[]{:S(2)}) async-start(), calls=%async_computation | async-start | bytes 3145728 | tf_op jit(solution)/shard_map/psum | solution.py:65
  7.3 4.0 copy-start.2
  9.2 6.1 copy-start.64
  11.2 4.1 copy-start.68
  11.2 161.0 %copy-start.54 = (f32[768]{0:T(1024)}, f32[768]{0:T(1024)S(1)}, u32[]{:S(2)}) copy-start(f32[768]{0:T(1024)S(1)} %get-tuple-element.86) | copy-start | bytes 9220
  11.2 160.9 %copy-start.76 = (f32[768]{0:T(1024)}, f32[768]{0:T(1024)S(1)}, u32[]{:S(2)}) copy-start(f32[768]{0:T(1024)S(1)} %get-tuple-element.55) | copy-start | bytes 9220
  11.3 297.5 %copy-start.56 = (f32[768]{0:T(1024)}, f32[768]{0:T(1024)S(1)}, u32[]{:S(2)}) copy-start(f32[768]{0:T(1024)S(1)} %get-tuple-element.54) | copy-start | bytes 9220
  16.7 5.2 copy-start.70
  19.3 5.2 copy-start.24
  31.6 120.0 %all-reduce.14.cloned.1.call-start = ((), (), s32[]{:S(2)}) async-start(), calls=%async_computation.1 | async-start | bytes 3145728 | tf_op jit(solution)/shard_map/psum | solution.py:71
  88.8 3.6 copy-start.62
  99.9 202.9 %all-reduce.16.cloned.1.call-start = ((), (), s32[]{:S(2)}) async-start(), calls=%async_computation.2 | async-start | bytes 6291456 | tf_op jit(solution)/shard_map/psum | solution.py:65
  100.3 51.2 %copy-start.75 = (f32[768]{0:T(1024)S(1)}, f32[768]{0:T(1024)}, u32[]{:S(2)}) copy-start(f32[768]{0:T(1024)} %param.12) | copy-start | bytes 9220
  171.1 8.9 copy-start.58
  172.2 7.8 copy-start.60
  180.3 10.9 copy-start.16
  180.4 10.9 copy-start.18
  180.4 21.0 %copy-start.27 = (bf16[1,4,512,384]{2,3,0,1:T(8,128)(2,1)}, bf16[1,4,512,384]{2,3,0,1:T(8,128)(2,1)S(1)}, u32[]{:S(2)}) copy-start(bf16[1,4,512,384]{2,3,0,1:T(8,128)(2,1)S(1)} %get-tuple-element.74) | copy-start | bytes 4718596
  201.4 11.9 %copy-start.36 = (bf16[384,768]{1,0:T(8,128)(2,1)S(1)}, bf16[384,768]{1,0:T(8,128)(2,1)}, u32[]{:S(2)}) copy-start(bf16[384,768]{1,0:T(8,128)(2,1)} %param.14) | copy-start | bytes 1769476
  216.8 211.3 %all-reduce.18.cloned.1.call-start = ((), (), s32[]{:S(2)}) async-start(), calls=%async_computation.3 | async-start | bytes 6291456 | tf_op jit(solution)/shard_map/psum | solution.py:111
  307.8 126.7 %copy-start.46 = (f32[4,512]{1,0:T(4,128)}, f32[4,512]{1,0:T(4,128)S(1)}, u32[]{:S(2)}) copy-start(f32[4,512]{1,0:T(4,128)S(1)} %broadcast_multiply_fusion.4) | copy-start | bytes 24580
  311.3 123.2 %copy-start.48 = (f32[4,512]{1,0:T(4,128)}, f32[4,512]{1,0:T(4,128)S(1)}, u32[]{:S(2)}) copy-start(f32[4,512]{1,0:T(4,128)S(1)} %add_rsqrt_fusion) | copy-start | bytes 24580
  311.3 8.6 copy-start.32
  342.2 268.6 %all-reduce.20.cloned.1.call-start = ((), (), s32[]{:S(2)}) async-start(), calls=%async_computation.4 | async-start | bytes 6291456 | tf_op jit(solution)/shard_map/psum | solution.py:143
  428.2 6.4 copy-start.23
  428.2 6.4 copy-start.33
  459.5 21.9 %copy-start.19 = (bf16[1,4,512,384]{2,3,0,1:T(8,128)(2,1)S(1)}, bf16[1,4,512,384]{2,3,0,1:T(8,128)(2,1)}, u32[]{:S(2)}) copy-start(bf16[1,4,512,384]{2,3,0,1:T(8,128)(2,1)} %copy-done.18) | copy-start | bytes 4718596
  476.9 4.6 copy-start.8
  524.9 173.8 %all-reduce.22.cloned.1.call-start = ((), (), s32[]{:S(2)}) async-start(), calls=%async_computation.5 | async-start | bytes 3145728 | tf_op jit(solution)/shard_map/psum | solution.py:111
  525.6 85.2 %copy-start.55 = (f32[768]{0:T(1024)S(1)}, f32[768]{0:T(1024)}, u32[]{:S(2)}) copy-start(f32[768]{0:T(1024)} %copy-done.54) | copy-start | bytes 9220
  525.6 85.2 %copy-start.59 = (f32[4,512]{1,0:T(4,128)S(1)}, f32[4,512]{1,0:T(4,128)}, u32[]{:S(2)}) copy-start(f32[4,512]{1,0:T(4,128)} %copy-done.58) | copy-start | bytes 24580
  525.6 85.2 %copy-start.61 = (f32[4,512]{1,0:T(4,128)S(1)}, f32[4,512]{1,0:T(4,128)}, u32[]{:S(2)}) copy-start(f32[4,512]{1,0:T(4,128)} %copy-done.60) | copy-start | bytes 24580
  610.8 6.7 copy-start.20
  624.6 7.1 slice-start.8
  631.7 6.0 copy-start.22
  637.7 5.6 copy-start.83
  637.7 5.6 copy-start.80
  647.0 51.6 %copy-start.63 = (f32[4,256]{1,0:T(4,128)S(1)}, f32[4,256]{1,0:T(4,128)}, u32[]{:S(2)}) copy-start(f32[4,256]{1,0:T(4,128)} %copy-done.62) | copy-start | bytes 12292
  647.0 51.6 %copy-start.67 = (f32[4,256]{1,0:T(4,128)S(1)}, f32[4,256]{1,0:T(4,128)}, u32[]{:S(2)}) copy-start(f32[4,256]{1,0:T(4,128)} %copy-done.66) | copy-start | bytes 12292
  647.1 211.7 %all-reduce.26.cloned.1.call-start = ((), (), s32[]{:S(2)}) async-start(), calls=%async_computation.7 | async-start | bytes 9437184 | tf_op jit(solution)/shard_map/psum | solution.py:71
  698.7 3.8 copy-start.28
  710.4 7.2 slice-start
  710.4 7.2 slice-start.1
  717.6 4.5 copy-start.25
  727.6 4.7 copy-start.34
  739.1 6.7 copy-start.47
  739.1 6.7 copy-start.49
  739.1 384.8 %all-reduce.24.cloned.1.call-start = ((), (), s32[]{:S(2)}) async-start(), calls=%async_computation.6 | async-start | bytes 28311552 | tf_op jit(solution)/shard_map/psum | solution.py:183
  739.7 19.6 %slice-start.4 = ((s8[6291456]{0:T(1024)(128)(4,1)}), s8[4194304]{0:T(1024)(128)(4,1)S(1)}, s32[]{:S(2)}) async-start(s8[6291456]{0:T(1024)(128)(4,1)} %bitcast.181), calls=%async_computation.12 | async-start | bytes 8388608
  745.8 12.7 %copy-start.11 = (f32[4,256,768]{2,1,0:T(8,128)S(1)}, f32[4,256,768]{2,1,0:T(8,128)}, u32[]{:S(2)}) copy-start(f32[4,256,768]{2,1,0:T(8,128)} %copy-done.10) | copy-start | bytes 9437188
  745.8 12.7 %copy-start.42 = (bf16[4,6,64,256]{3,2,1,0:T(8,128)(2,1)S(1)}, bf16[4,6,64,256]{3,2,1,0:T(8,128)(2,1)}, u32[]{:S(2)}) copy-start(bf16[4,6,64,256]{3,2,1,0:T(8,128)(2,1)} %copy-done.41) | copy-start | bytes 2359300
  745.8 13.5 %slice-start.5 = ((s8[6291456]{0:T(1024)(128)(4,1)}), s8[2097152]{0:T(1024)(128)(4,1)S(1)}, s32[]{:S(2)}) async-start(s8[6291456]{0:T(1024)(128)(4,1)} %bitcast.181), calls=%async_computation.13 | async-start | bytes 4194304
  760.0 5.3 slice-start.2
  762.4 3.6 copy-start.39
  926.0 6.4 copy-start.6
  926.0 6.4 copy-start.12
  926.0 7.4 copy-start.21
  926.0 7.8 copy-start.30
  1123.9 5.3 copy-start.40
  1129.1 6.5 slice-start.6
  1130.1 5.5 slice-start.7
  (39 other events, 93.2 us)
Sparse Core Ops, SparseCore 0:
  31.7 54.1 all-reduce.11
  100.0 51.4 all-reduce.13
  217.0 85.7 all-reduce.15
  342.4 85.7 all-reduce.17
  525.0 85.7 all-reduce.19
  647.2 51.4 all-reduce.21
  739.2 119.5 all-reduce.25
  864.6 259.2 all-reduce.23
where the time goes:
time: 1150 us
  waiting for transfers between devices  658 us (57%)
  matrix products  226 us (20%)
  other arithmetic  104 us (9%)
  local copies, waits for them, and re-layouts  77 us (7%)
  blocking collectives  64.2 us (6%)
  between operations  15.8 us (1%)
    psum x1, waiting for transfers between devices, shards(): lax.psum((merged[0], merged[1], merged[2], merged[3], merged[4], merged[5...  187 us
    psum x2, waiting for transfers between devices, forward_block(): lax.psum(attn_term.astype(jnp.bfloat16), 'tensor').astype(jnp.float32)  140 us
    psum x2, waiting for transfers between devices, forward_block(): lax.psum(down_term.astype(jnp.bfloat16), 'tensor').astype(jnp.float32)  132 us
    psum x2, waiting for transfers between devices, backward_block(): lax.psum(up_term.astype(jnp.bfloat16), 'tensor').astype(jnp.float32)  125 us
    psum x1, waiting for transfers between devices, backward_block(): lax.psum(qkv_term.astype(jnp.bfloat16), 'tensor').astype(jnp.float32)  73.4 us
    psum x1, blocking collectives, shards(): lax.psum((merged[0], merged[1], merged[2], merged[3], merged[4], merged[5...  64.2 us
    unnamed x195, local copies, waits for them, and re-layouts  37.5 us
    dot_general x2, matrix products, backward_block(): jnp.einsum('rqhe,rkhe->rhqk', grad_att, head_view[2], preferred_element_t...  24.2 us
  transfers between devices with their start and end apart: 8, of which 8 were waited for; matrix products, arithmetic and copies ran while one was open for 6% of the time, Pallas kernels for 0%

commit v1 on v0

v1 whole, which is shorter than its diff:
```python
import jax
import jax.numpy as jnp
from jax import lax
from jax.sharding import Mesh
from jax.sharding import PartitionSpec as P

HD = 64
EPS = 1e-05
NEG = -1000000000.0
F32 = jnp.float32
BF16 = jnp.bfloat16
ROWS_OVER = ("o", "x", "core")
FLIP = ((0, 1), (1, 0))


def ordered(flag, mine, theirs):
    first = flag == 0
    return jnp.stack([jnp.where(first, mine, theirs), jnp.where(first, theirs, mine)])


def take_half(array, index):
    half = array.shape[0] // 2
    return lax.dynamic_slice_in_dim(array, index * half, half, 0)


def flip_bit(array, axis, size, bit):
    return lax.ppermute(array, axis, [(i, i ^ bit) for i in range(size)])


def steps_of(outer):
    steps = [("x", 2, 1)]
    bit = 1
    while bit < outer:
        steps.append(("o", outer, bit))
        bit *= 2
    return steps


def my_bit(axis, bit):
    return (lax.axis_index(axis) // bit) % 2


def fetch_half(own):
    shape = own.shape
    flat = own.reshape(-1, shape[-1])
    x, core = lax.axis_index("x"), lax.axis_index("core")
    piece = take_half(take_half(flat, core), x)
    got = lax.ppermute(piece, "tensor", FLIP)
    got = ordered(x, got, lax.ppermute(got, "x", FLIP)).reshape(-1, shape[-1])
    got = ordered(core, got, lax.ppermute(got, "core", FLIP)).reshape(shape)
    return got


def reduce_grad(own, other, outer):
    core = lax.axis_index("core")
    other_low = other.astype(BF16)
    own_low = own.astype(BF16)
    sent = lax.ppermute(take_half(other_low, 1 - core), "core", FLIP)
    other_sum = take_half(other, core) + sent.astype(F32)
    sent = lax.ppermute(take_half(own_low, 1 - core), "core", FLIP)
    total = take_half(own, core) + sent.astype(F32)
    total = total + lax.ppermute(other_sum.astype(BF16), "tensor", FLIP).astype(F32)
    steps = steps_of(outer)
    for axis, size, bit in steps:
        mine = my_bit(axis, bit)
        low = take_half(total.astype(BF16), 1 - mine)
        total = take_half(total, mine) + flip_bit(low, axis, size, bit).astype(F32)
    whole = total.astype(BF16)
    for axis, size, bit in reversed(steps):
        got = flip_bit(whole, axis, size, bit)
        whole = ordered(my_bit(axis, bit), whole, got).reshape(-1, whole.shape[-1])
    got = lax.ppermute(whole, "core", FLIP)
    whole = ordered(core, whole, got).reshape(-1, whole.shape[-1])
    return whole.astype(F32)


def sum_small(small, outer):
    for axis, size, bit in [("core", 2, 1), ("tensor", 2, 1)] + steps_of(outer):
        small = small + flip_bit(small, axis, size, bit)
    return small


def norm_parts(act, gain, bias):
    centred = act - jnp.mean(act, axis=-1, keepdims=True)
    inverse = lax.rsqrt(jnp.mean(centred * centred, axis=-1, keepdims=True) + EPS)
    normal = centred * inverse
    return (normal * gain + bias).astype(BF16), normal, inverse


def norm_back(grad, normal, inverse, gain):
    scaled = grad * gain
    centre = jnp.mean(scaled, axis=-1, keepdims=True)
    proj = jnp.mean(scaled * normal, axis=-1, keepdims=True)
    return inverse * (scaled - centre - normal * proj)


def mm(spec, a, b):
    return jnp.einsum(spec, a, b, preferred_element_type=F32)


def gelu(values):
    return jax.nn.gelu(values, approximate=True)


def attend(q, k, v, visible):
    s = mm("hrqe,hrke->hrqk", q, k) * HD**-0.5
    s = jnp.where(visible, s, NEG)
    top = jnp.max(s, axis=-1, keepdims=True)
    e = jnp.exp(s - top)
    mass = jnp.sum(e, axis=-1, keepdims=True)
    o = mm("hrqk,hrke->hrqe", (e / mass).astype(BF16), v)
    return o.astype(BF16), top + jnp.log(mass)


def attend_back(q, k, v, do, visible, lse):
    s = mm("hrqe,hrke->hrqk", q, k) * HD**-0.5
    s = jnp.where(visible, s, NEG)
    p = jnp.exp(s - lse)
    dv = mm("hrqk,hrqe->hrke", p.astype(BF16), do)
    dp = mm("hrqe,hrke->hrqk", do, v)
    ds = (p * (dp - jnp.sum(dp * p, axis=-1, keepdims=True))).astype(BF16)
    dq = mm("hrqk,hrke->hrqe", ds, k) * HD**-0.5
    dk = mm("hrqk,hrqe->hrke", ds, q) * HD**-0.5
    return dq, dk, dv


def split_heads(t):
    r, n, d = t.shape
    return t.reshape(r, n, d // HD, HD).transpose(2, 0, 1, 3)


def join_heads(t):
    h, r, n, e = t.shape
    return t.transpose(1, 2, 0, 3).reshape(r, n, h * e)


def shards(outer, tokens, segments, pass_embed, w_qkv, w_out, w_up, w_down, gain, bias, cotangent):
    ty = lax.axis_index("tensor")
    rows = tokens.shape[0] // 2
    seq, width = tokens.shape[1], tokens.shape[2]
    mine = lambda t: lax.dynamic_slice_in_dim(t, ty * rows, rows, 0)
    x = mine(tokens).astype(F32)
    seg = mine(segments)
    cot = mine(cotangent).reshape(rows, seq, 2, width).transpose(0, 2, 1, 3).reshape(rows, 2 * seq, width)
    wqkv = jnp.concatenate([w_qkv, fetch_half(w_qkv)], axis=2)
    wout = jnp.concatenate([w_out, fetch_half(w_out)], axis=0)
    wup = jnp.concatenate([w_up, fetch_half(w_up)], axis=1)
    wdown = jnp.concatenate([w_down, fetch_half(w_down)], axis=0)

    place = jnp.arange(seq, dtype=jnp.int32)
    same = seg[:, :, None] == seg[:, None, :]
    vis_one = (same & (place[:, None] >= place[None, :])[None])[None]
    place2 = jnp.concatenate([2 * place, 2 * place + 1])
    seg2 = jnp.concatenate([seg, seg], axis=1)
    vis_two = ((seg2[:, :, None] == seg2[:, None, :]) & (place2[:, None] >= place2[None, :])[None])[None]

    def project(a):
        return [split_heads(mm("rld,de->rle", a, wqkv[j]).astype(BF16)) for j in range(3)]

    def rest(h, o):
        h1 = h + mm("rle,ed->rld", o, wout)
        n2, hat2, inv2 = norm_parts(h1, gain[1], bias[1])
        u = mm("rld,df->rlf", n2, wup)
        g = gelu(u).astype(BF16)
        z = h1 + mm("rlf,fd->rld", g, wdown)
        return z, (o, n2, hat2, inv2, u, g)

    def rest_back(db, kept):
        o, n2, hat2, inv2, u, g = kept
        dm = db.astype(BF16)
        dg = mm("rld,fd->rlf", dm, wdown)
        du = jax.vjp(gelu, u)[1](dg)[0].astype(BF16)
        dn2 = mm("rlf,df->rld", du, wup)
        dh1 = db + norm_back(dn2, hat2, inv2, gain[1])
        dp = dh1.astype(BF16)
        do = split_heads(mm("rld,ed->rle", dp, wout).astype(BF16))
        grads = (jnp.sum(dn2 * hat2, axis=(0, 1)), jnp.sum(dn2, axis=(0, 1)))
        return dh1, do, (g, dm, n2, du, o, dp), grads

    a_e, hat_e, inv_e = norm_parts(x, gain[0], bias[0])
    qkv_e = project(a_e)
    o1, lse1 = attend(*qkv_e, vis_one)
    y, kept1 = rest(x, join_heads(o1))
    h_o = y + pass_embed
    a_o, hat_o, inv_o = norm_parts(h_o, gain[0], bias[0])
    qkv_o = project(a_o)
    both = [jnp.concatenate([e, o], axis=2) for e, o in zip(qkv_e, qkv_o)]
    o2, lse2 = attend(*both, vis_two)
    u2 = jnp.concatenate([x, h_o], axis=1)
    z, kept2 = rest(u2, join_heads(o2))
    out_mine = z.astype(BF16).reshape(rows, 2, seq, width).transpose(0, 2, 1, 3).reshape(rows, 2 * seq, width)
    out = ordered(ty, out_mine, lax.ppermute(out_mine, "tensor", FLIP)).reshape(cotangent.shape)

    dh1_2, do2, terms2, ln2 = rest_back(cot.astype(F32), kept2)
    dqkv2 = attend_back(*both, do2, vis_two, lse2)

    def back_project(d):
        return sum(mm("rle,de->rld", d[j], wqkv[j]) for j in range(3))

    d_o = [join_heads(t[:, :, seq:]).astype(BF16) for t in dqkv2]
    da_o = back_project(d_o)
    dy = dh1_2[:, seq:] + norm_back(da_o, hat_o, inv_o, gain[0])

    dh1_1, do1, terms1, ln1 = rest_back(dy, kept1)
    dqkv1 = attend_back(*qkv_e, do1, vis_one, lse1)
    d_e = [join_heads(t[:, :, :seq] + s).astype(BF16) for t, s in zip(dqkv2, dqkv1)]
    da_e = back_project(d_e)
    grad_tokens = dh1_1 + dh1_2[:, :seq] + norm_back(da_e, hat_e, inv_e, gain[0])
    gt = grad_tokens.astype(BF16)
    gt = ordered(ty, gt, lax.ppermute(gt, "tensor", FLIP)).reshape(tokens.shape).astype(F32)

    def wgrad(i, j):
        one = mm("rla,rlb->ab", terms1[i], terms1[j])
        return one + mm("rla,rlb->ab", terms2[i], terms2[j])

    half = lambda t, axis: jnp.split(t, 2, axis=axis)
    g_down = reduce_grad(*half(wgrad(0, 1), 0), outer)
    g_up = reduce_grad(*half(wgrad(2, 3), 1), outer)
    g_out = reduce_grad(*half(wgrad(4, 5), 0), outer)
    gq = jnp.stack([mm("rla,rlb->ab", a_e, e) + mm("rla,rlb->ab", a_o, o) for e, o in zip(d_e, d_o)])
    g_qkv = reduce_grad(*[t.reshape(3 * width, -1) for t in half(gq, 2)], outer).reshape(3, width, -1)

    small = jnp.stack(
        [
            jnp.sum(da_e * hat_e, axis=(0, 1)) + jnp.sum(da_o * hat_o, axis=(0, 1)),
            ln1[0] + ln2[0],
            jnp.sum(da_e, axis=(0, 1)) + jnp.sum(da_o, axis=(0, 1)),
            ln1[1] + ln2[1],
            jnp.sum(dy, axis=(0, 1)),
        ]
    )
    small = sum_small(small, outer)
    return out, gt, g_qkv, g_out, g_up, g_down, small[0:2], small[2:4], small[4]


def solution(mesh):
    outer = mesh.shape["dp"] // 4
    fine = Mesh(mesh.devices.reshape(outer, 2, 2, mesh.shape["tensor"]), ("o", "x", "core", "tensor"))
    rows = ROWS_OVER
    placed = (
        P(rows, None, None),
        P(rows, None),
        P(),
        P(None, None, "tensor"),
        P("tensor", None),
        P(None, "tensor"),
        P("tensor", None),
        P(),
        P(),
        P(rows, None, None),
    )

    def body(*args):
        return shards(outer, *args)

    return jax.shard_map(
        body,
        mesh=fine,
        in_specs=placed,
        out_specs=(
            P(rows, None, None),
            P(rows, None, None),
            P(None, None, "tensor"),
            P("tensor", None),
            P(None, "tensor"),
            P("tensor", None),
            P(),
            P(),
            P(),
        ),
        check_vma=False,
    )
```

time: 1150 us -> 694 us (0.60)
  waiting for transfers between devices: 658 us -> 200 us
  starting transfers between devices: 0.72 us -> 71 us
  blocking collectives: 64.2 us -> 0 us
  between operations: 15.8 us -> 3.56 us
    psum x8 -> x0, waiting for transfers between devices: 657 us -> none  [the longest x1 187 us: shards(): lax.psum((merged[0], merged[1], merged[2], merged[3], merged[4], merged[5...]
    ppermute x0 -> x59, waiting for transfers between devices: none -> 200 us  [the longest x29 75 us: flip_bit(): return lax.ppermute(array, axis, [(i, i ^ bit) for i in range(size)])]
    ppermute x0 -> x59, starting transfers between devices: none -> 71 us  [the longest x29 50.6 us: flip_bit(): return lax.ppermute(array, axis, [(i, i ^ bit) for i in range(size)])]
    psum x1 -> x0, blocking collectives: 64.2 us -> none  [shards(): lax.psum((merged[0], merged[1], merged[2], merged[3], merged[4], merged[5...]
    reduce_sum x14 -> x8, other arithmetic: 47.7 us -> 15.7 us  [the longest x2 12.2 us: attend(): mass = jnp.sum(e, axis=-1, keepdims=True)]
    another operation x15 -> x3, local copies, waits for them, and re-layouts: 23.1 us -> 2.11 us  [the longest x1 2.07 us: ordered(): jnp.stack([jnp.where(first, mine, theirs), jnp.where(first, theirs, mine)])]
    convert_element_type x1 -> x39, local copies, waits for them, and re-layouts: 1.4 us -> 22.1 us  [the longest x6 9.05 us: project(): mm('rld,de->rle', a, wqkv[j]).astype(BF16)]
    convert_element_type x3 -> x18, other arithmetic: 28.1 us -> 43.2 us  [the longest x2 24.2 us: attend_back(): ds = (p * (dp - jnp.sum(dp * p, axis=-1, keepdims=True))).astype(BF16)]
  transfers between devices with their start and end apart: 8 -> 59, of which waited for: 8 -> 32; matrix products, arithmetic and copies ran while one was open for 6% -> 18% of each run, Pallas kernels for 0% -> 0%
where the time goes in v1:
time: 694 us; the launch traced here: 687 us
  matrix products  234 us (34%)
  waiting for transfers between devices  200 us (29%)
  other arithmetic  94.5 us (14%)
  local copies, waits for them, and re-layouts  83.5 us (12%)
  starting transfers between devices  71 us (10%)
    dot_general x48, matrix products, mm(): return jnp.einsum(spec, a, b, preferred_element_type=F32)  234 us
    ppermute x29, waiting for transfers between devices, flip_bit(): return lax.ppermute(array, axis, [(i, i ^ bit) for i in range(size)])  75 us
    ppermute x29, starting transfers between devices, flip_bit(): return lax.ppermute(array, axis, [(i, i ^ bit) for i in range(size)])  50.6 us
    ppermute x4, waiting for transfers between devices, reduce_grad(): lax.ppermute(other_sum.astype(BF16), 'tensor', FLIP).astype(F32)  40.7 us
    ppermute x4, waiting for transfers between devices, fetch_half(): got = ordered(x, got, lax.ppermute(got, 'x', FLIP)).reshape(-1, shape[-1])  31.8 us
    ppermute x1, waiting for transfers between devices, shards(): lax.ppermute(out_mine, 'tensor', FLIP)  29.3 us
    unnamed x272, local copies, waits for them, and re-layouts  27.3 us
    convert_element_type x2, other arithmetic, attend_back(): ds = (p * (dp - jnp.sum(dp * p, axis=-1, keepdims=True))).astype(BF16)  24.2 us
  transfers between devices with their start and end apart: 59, of which 32 were waited for; matrix products, arithmetic and copies ran while one was open for 18% of the time, Pallas kernels for 0%

profile of v1, /device:TPU:0, one launch (start us, length us, event | category | flops | bytes accessed | tf_op | source)
XLA Modules:
  0.0 687.2 jit_solution(11432595757681112726)
XLA Ops:
  2.9 3.0 collective-permute-start.6
  17.0 15.8 %collective-permute-done.3 = bf16[96,768]{1,0:T(8,128)(2,1)S(1)} collective-permute-done((bf16[96,768]{1,0:T(8,128)(2,1)S(1)}, bf16[96,768]{1,0:T(8,128)(2,1)S(1)}, u32[]{:S(2)}, u32[]{:S(2)}) %collective-permute-start.3) | collective-permute-done | bytes 147488 | tf_op jit(solution)/shard_map/ppermute | solution.py:48
  34.9 3.1 collective-permute-done.4
  39.4 3.0 copy.128
  51.8 7.2 %collective-permute-done.1 = bf16[576,384]{1,0:T(8,128)(2,1)S(1)} collective-permute-done((bf16[576,384]{1,0:T(8,128)(2,1)}, bf16[576,384]{1,0:T(8,128)(2,1)S(1)}, u32[]{:S(2)}, u32[]{:S(2)}) %collective-permute-start.1) | collective-permute-done | bytes 442400 | tf_op jit(solution)/shard_map/ppermute | solution.py:49
  60.2 11.3 %collective-permute-done.7 = bf16[192,1536]{1,0:T(8,128)(2,1)S(1)} collective-permute-done((bf16[192,1536]{1,0:T(8,128)(2,1)}, bf16[192,1536]{1,0:T(8,128)(2,1)S(1)}, u32[]{:S(2)}, u32[]{:S(2)}) %collective-permute-start.7) | collective-permute-done | bytes 589856 | tf_op jit(solution)/shard_map/ppermute | solution.py:49
  73.8 10.2 %collective-permute-done.10 = bf16[384,768]{1,0:T(8,128)(2,1)S(1)} collective-permute-done((bf16[384,768]{1,0:T(8,128)(2,1)}, bf16[384,768]{1,0:T(8,128)(2,1)S(1)}, u32[]{:S(2)}, u32[]{:S(2)}) %collective-permute-start.10) | collective-permute-done | bytes 589856 | tf_op jit(solution)/shard_map/ppermute | solution.py:49
  92.2 3.2 convolution_convert_fusion.6
  96.8 3.4 convolution_convert_fusion.5
  113.5 2.6 select_bitcast_fusion.5
  118.6 2.7 fusion.73
  121.4 4.1 fusion.96
  142.7 12.3 %fusion.13 = (f32[12,2,512]{2,1,0:T(2,128)S(1)}, f32[12,2,512,512]{2,3,1,0:T(8,128)}) fusion(pred[2,512,512]{1,2,0:T(8,128)(4,1)S(1)} %copy-done.19, bf16[12,2,256,64]{2,3,1,0:T(8,128)(2,1)} %bitcast.419, bf16[12,2,256,64]{2,3,1,0:T(8,128)(2,1)S(1)} %bitcast.413, bf16[12,2,256,64]{2,3,1,0:T(8,128)(2,1)} %bitcast.417, bf16[12,2,256,64]{2,3,1,0:T(8,128)(2,1)} %bitcast.415), kind=kOutput, calls=%fused_computation.25 | convolution fusion | flops 830459904 | bytes 28884992 | tf_op jit(solution)/shard_map/hrqe,hrke->hrqk/dot_general | solution.py:98
  155.0 11.1 %fusion = f32[12,2,512]{2,1,0:T(2,128)S(1)} fusion(f32[12,2,512]{2,1,0:T(2,128)S(1)} %get-tuple-element.102, f32[12,2,512,512]{2,3,1,0:T(8,128)} %get-tuple-element.103, pred[2,512,512]{1,2,0:T(8,128)(4,1)S(1)} %copy-done.19), kind=kLoop, calls=%fused_computation.6 | loop fusion | flops 25153536 | bytes 25788416 | tf_op jit(solution)/shard_map/reduce_sum | solution.py:110
  166.2 12.4 %fusion.40 = bf16[2,512,12,64]{1,3,0,2:T(8,128)(2,1)S(1)} fusion(f32[12,2,512]{2,1,0:T(2,128)S(1)} %fusion, f32[12,2,512]{2,1,0:T(2,128)S(1)} %get-tuple-element.102, f32[12,2,512,512]{2,3,1,0:T(8,128)} %get-tuple-element.103, pred[2,512,512]{1,2,0:T(8,128)(4,1)S(1)} %copy-done.19, bf16[12,2,256,64]{2,3,1,0:T(8,128)(2,1)S(1)} %bitcast.433, ...), kind=kOutput, calls=%fused_computation.133 | convolution fusion | flops 840695808 | bytes 28934144 | tf_op jit(solution)/shard_map/hrqk,hrke->hrqe/dot_general | solution.py:98
  185.2 8.2 %fusion.71 = f32[2,512,3072]{2,1,0:T(8,128)} fusion(f32[2,512,768]{2,1,0:T(8,128)S(1)} %get-tuple-element.105, f32[768]{0:T(1024)S(1)} %get-tuple-element.27, f32[768]{0:T(1024)S(1)} %get-tuple-element.117, f32[2,512]{1,0:T(2,128)S(1)} %add_rsqrt_fusion, f32[2,512]{1,0:T(2,128)S(1)} %broadcast_multiply_fusion.2, bf16[768,1536]{1,0:T(8,128)(2,1)S(1)} %bitcast.444, ...), kind=kOutput, calls=%fused_computation.286 | convolution fusion | flops 4845207552 | bytes 20461568 | tf_op jit(solution)/shard_map/rld,df->rlf/dot_general | solution.py:98
  193.4 15.9 %fusion.8 = bf16[2,512,3072]{2,1,0:T(8,128)(2,1)S(1)} fusion(f32[2,512,3072]{2,1,0:T(8,128)} %fusion.71, bf16[2,512,768]{2,1,0:T(8,128)(2,1)S(1)} %bitcast.404, bf16[1536,768]{1,0:T(8,128)(2,1)S(1)} %bitcast.439, bf16[1536,768]{1,0:T(8,128)(2,1)} %param.16), kind=kOutput, calls=%fused_computation.16 | convolution fusion | flops 4904189952 | bytes 25165824 | tf_op jit(solution)/shard_map/rld,fd->rlf/dot_general | solution.py:98
  209.4 10.4 %multiply_reduce_fusion.2 = (f32[768]{0:T(1024)S(1)}, f32[2,512]{1,0:T(2,128)S(1)}, f32[2,512]{1,0:T(2,128)S(1)}, f32[768]{0:T(1024)S(1)}, f32[2,512,768]{2,1,0:T(8,128)S(1)}) fusion(f32[2,512,768]{2,1,0:T(8,128)S(1)} %get-tuple-element.105, f32[2,512]{1,0:T(2,128)S(1)} %add_rsqrt_fusion, f32[2,512]{1,0:T(2,128)S(1)} %broadcast_multiply_fusion.2, ...), kind=kOutput, calls=%fused_computation.52 | convolution fusion | flops 4848349184 | bytes 17327104 | tf_op jit(solution)/shard_map/rlf,df->rld/dot_general | solution.py:98
  223.9 2.6 copy.130
  226.5 17.7 %multiply_reduce_fusion = (f32[12,2,512]{2,1,0:T(2,128)S(1)}, f32[12,2,512,512]{2,3,1,0:T(8,128)}) fusion(f32[12,2,512]{2,1,0:T(2,128)S(1)} %bitcast.464, f32[12,2,512,512]{2,3,1,0:T(8,128)} %get-tuple-element.103, pred[2,512,512]{1,2,0:T(8,128)(4,1)} %compare_and_fusion, bf16[12,2,256,64]{2,3,1,0:T(8,128)(2,1)} %bitcast.434, ...), kind=kOutput, calls=%fused_computation.1 | convolution fusion | flops 839897088 | bytes 54099968 | tf_op jit(solution)/shard_map/hrqe,hrke->hrqk/dot_general | solution.py:98
  244.2 22.5 %multiply_convert_fusion = bf16[12,2,512,512]{2,3,1,0:T(8,128)(2,1)} fusion(f32[12,2,512,512]{2,3,1,0:T(8,128)} %get-tuple-element.108, f32[12,2,512]{2,1,0:T(2,128)S(1)} %get-tuple-element.107, f32[12,2,512]{2,1,0:T(2,128)S(1)} %bitcast.465, f32[12,2,512,512]{2,3,1,0:T(8,128)} %get-tuple-element.103, pred[2,512,512]{1,2,0:T(8,128)(4,1)} %compare_and_fusion), kind=kLoop, calls=%fused_computation | loop fusion | flops 37748736 | bytes 63537152 | tf_op jit(solution)/shard_map/convert_element_type | solution.py:121
  266.7 10.5 %convolution_multiply_fusion.1 = f32[12,2,512,64]{2,3,1,0:T(8,128)} fusion(bf16[12,2,512,512]{2,3,1,0:T(8,128)(2,1)} %multiply_convert_fusion, bf16[12,2,256,64]{2,3,1,0:T(8,128)(2,1)} %bitcast.418, bf16[12,2,256,64]{2,3,1,0:T(8,128)(2,1)} %bitcast.416), kind=kOutput, calls=%fused_computation.87 | convolution fusion | flops 809238528 | bytes 17301504 | tf_op jit(solution)/shard_map/hrqk,hrqe->hrke/dot_general | solution.py:98
  277.2 7.2 %convolution_multiply_fusion = f32[12,2,512,64]{2,3,1,0:T(8,128)S(1)} fusion(bf16[12,2,512,512]{2,3,1,0:T(8,128)(2,1)} %multiply_convert_fusion, bf16[12,2,256,64]{2,3,1,0:T(8,128)(2,1)} %bitcast.420, bf16[12,2,256,64]{2,3,1,0:T(8,128)(2,1)} %bitcast.414), kind=kOutput, calls=%fused_computation.86 | convolution fusion | flops 809238528 | bytes 17301504 | tf_op jit(solution)/shard_map/hrqk,hrke->hrqe/dot_general | solution.py:98
  284.3 14.0 %fusion.9 = f32[12,2,512,64]{2,3,1,0:T(8,128)} fusion(f32[12,2,512]{2,1,0:T(2,128)S(1)} %bitcast.466, f32[12,2,512,512]{2,3,1,0:T(8,128)} %get-tuple-element.103, pred[2,512,512]{1,2,0:T(8,128)(4,1)S(1)} %copy-done.20, bf16[12,2,512,64]{2,3,0,1:T(8,128)(2,1)} %bitcast.402), kind=kOutput, calls=%fused_computation.17 | convolution fusion | flops 830472192 | bytes 30457856 | tf_op jit(solution)/shard_map/hrqk,hrqe->hrke/dot_general | solution.py:98
  310.1 10.4 %fusion.20 = bf16[2,256,3072]{2,1,0:T(8,128)(2,1)S(1)} fusion(f32[2,256,3072]{2,1,0:T(8,128)} %copy-done.127, f32[2,256,768]{2,1,0:T(8,128)S(1)} %get-tuple-element.30, bf16[1536,768]{1,0:T(8,128)(2,1)S(1)} %bitcast.440, bf16[1536,768]{1,0:T(8,128)(2,1)S(1)} %copy-done.95), kind=kOutput, calls=%fused_computation.33 | convolution fusion | flops 2457206784 | bytes 15728640 | tf_op jit(solution)/shard_map/rld,fd->rlf/dot_general | solution.py:98
  320.5 3.0 multiply_reduce_fusion.6
  327.9 4.6 multiply_reduce_fusion.1
  334.6 2.7 fusion.47
  340.8 9.7 %fusion.68 = f32[3072,768,1]{1,0,2:T(8,128)} fusion(f32[2,256,768]{2,1,0:T(8,128)S(1)} %copy-done.46, f32[2,256,3072]{2,1,0:T(8,128)} %copy-done.127), kind=kOutput, calls=%fused_computation.237 | convolution fusion | flops 2430468096 | bytes 17301504 | tf_op jit(solution)/shard_map/rla,rlb->ab/dot_general | solution.py:98
  350.8 5.7 fusion.72
  367.0 11.2 %add_convert_fusion = bf16[2,512,768]{2,1,0:T(8,128)(2,1)} fusion(f32[2,512,768]{2,1,0:T(8,128)S(1)} %copy-done.6, bf16[1536,768]{1,0:T(8,128)(2,1)S(1)} %bitcast.441, bf16[1536,768]{1,0:T(8,128)(2,1)S(1)} %copy-done.96, f32[2,512,3072]{2,1,0:T(8,128)} %fusion.71), kind=kOutput, calls=%fused_computation.56 | convolution fusion | flops 4871159808 | bytes 22020096 | tf_op jit(solution)/shard_map/rlf,fd->rld/dot_general | solution.py:98
  380.9 3.1 multiply_reduce_fusion.8
  384.7 14.6 %bitcast_add_fusion = f32[3072,768]{1,0:T(8,128)} fusion(f32[3072,768,1]{1,0,2:T(8,128)} %fusion.68, bf16[2,512,768]{2,1,0:T(8,128)(2,1)} %bitcast.403, f32[2,512,3072]{2,1,0:T(8,128)} %fusion.71), kind=kOutput, calls=%fused_computation.21 | convolution fusion | flops 4862509056 | bytes 33030144 | tf_op jit(solution)/shard_map/rla,rlb->ab/dot_general | solution.py:98
  399.3 4.4 fusion.89
  408.1 10.5 %bitcast_add_fusion.1 = f32[768,3072]{1,0:T(8,128)S(1)} fusion(f32[768,3072,1]{1,0,2:T(8,128)} %fusion.72, bf16[2,512,3072]{2,1,0:T(8,128)(2,1)} %copy-done.37, f32[2,512,768]{2,1,0:T(8,128)S(1)} %copy-done.6, f32[768]{0:T(1024)S(1)} %get-tuple-element.27, f32[768]{0:T(1024)S(1)} %get-tuple-element.117, f32[2,512]{1,0:T(2,128)S(1)} %copy-done.90, ...), kind=kOutput, calls=%fused_computation.22 | convolution fusion | flops 4838129664 | bytes 28325888 | tf_op jit(solution)/shard_map/rla,rlb->ab/dot_general | solution.py:98
  418.7 3.1 fusion.90
  422.3 3.1 bitcast_add_fusion.2
  449.4 2.8 collective-permute-start.58
  458.3 3.9 collective-permute-done.27
  466.7 7.5 %collective-permute-done.13 = bf16[2,256,768]{2,1,0:T(8,128)(2,1)S(1)} collective-permute-done((bf16[2,256,768]{2,1,0:T(8,128)(2,1)S(1)}, bf16[2,256,768]{2,1,0:T(8,128)(2,1)S(1)}, u32[]{:S(2)}, u32[]{:S(2)}) %collective-permute-start.13) | collective-permute-done | bytes 786464 | tf_op jit(solution)/shard_map/ppermute | solution.py:210
  474.2 2.8 collective-permute-start.29
  490.8 4.4 collective-permute-done.32
  498.9 2.6 add_convert_fusion.2
  503.2 29.3 %collective-permute-done.12 = bf16[2,512,768]{2,0,1:T(2,128)(2,1)S(1)} collective-permute-done((bf16[2,512,768]{2,0,1:T(2,128)(2,1)S(1)}, bf16[2,512,768]{2,0,1:T(2,128)(2,1)S(1)}, u32[]{:S(2)}, u32[]{:S(2)}) %collective-permute-start.12) | collective-permute-done | bytes 1572896 | tf_op jit(solution)/shard_map/ppermute | solution.py:192
  534.2 3.3 fusion.31
  538.0 13.6 %collective-permute-done.16 = bf16[1152,384]{1,0:T(8,128)(2,1)S(1)} collective-permute-done((bf16[1152,384]{1,0:T(8,128)(2,1)S(1)}, bf16[1152,384]{1,0:T(8,128)(2,1)S(1)}, u32[]{:S(2)}, u32[]{:S(2)}) %collective-permute-start.16) | collective-permute-done | bytes 884768 | tf_op jit(solution)/shard_map/ppermute | solution.py:62
  553.5 4.4 pad_maximum_fusion.1
  563.2 13.7 %collective-permute-done.46 = bf16[768,768]{1,0:T(8,128)(2,1)} collective-permute-done((bf16[768,768]{1,0:T(8,128)(2,1)}, bf16[768,768]{1,0:T(8,128)(2,1)}, u32[]{:S(2)}, u32[]{:S(2)}) %collective-permute-start.46) | collective-permute-done | bytes 1179680 | tf_op jit(solution)/shard_map/ppermute | solution.py:62
  583.2 2.8 collective-permute-done.19
  587.4 13.4 %collective-permute-done.36 = bf16[384,1536]{1,0:T(8,128)(2,1)S(1)} collective-permute-done((bf16[384,1536]{1,0:T(8,128)(2,1)}, bf16[384,1536]{1,0:T(8,128)(2,1)S(1)}, u32[]{:S(2)}, u32[]{:S(2)}) %collective-permute-start.36) | collective-permute-done | bytes 1179680 | tf_op jit(solution)/shard_map/ppermute | solution.py:62
  605.7 3.2 collective-permute-done.21
  612.2 8.3 %collective-permute-done.37 = bf16[192,1536]{1,0:T(8,128)(2,1)S(1)} collective-permute-done((bf16[192,1536]{1,0:T(8,128)(2,1)S(1)}, bf16[192,1536]{1,0:T(8,128)(2,1)S(1)}, u32[]{:S(2)}, u32[]{:S(2)}) %collective-permute-start.37) | collective-permute-done | bytes 589856 | tf_op jit(solution)/shard_map/ppermute | solution.py:27
  623.9 4.7 collective-permute-done.38
  628.7 2.9 collective-permute-start.39
  632.3 8.6 %collective-permute-done.39 = bf16[48,1536]{1,0:T(8,128)(2,1)S(1)} collective-permute-done((bf16[48,1536]{1,0:T(8,128)(2,1)S(1)}, bf16[48,1536]{1,0:T(8,128)(2,1)S(1)}, u32[]{:S(2)}, u32[]{:S(2)}) %collective-permute-start.39) | collective-permute-done | bytes 147488 | tf_op jit(solution)/shard_map/ppermute | solution.py:27
  641.0 3.0 collective-permute-done.50
  644.1 3.0 collective-permute-start.51
  647.6 2.9 collective-permute-start.41
  650.5 4.5 collective-permute-done.51
  656.7 3.0 collective-permute-done.41
  661.4 10.0 %collective-permute-done.52 = bf16[384,768]{1,0:T(8,128)(2,1)S(1)} collective-permute-done((bf16[384,768]{1,0:T(8,128)(2,1)S(1)}, bf16[384,768]{1,0:T(8,128)(2,1)S(1)}, u32[]{:S(2)}, u32[]{:S(2)}) %collective-permute-start.52) | collective-permute-done | bytes 589856 | tf_op jit(solution)/shard_map/ppermute | solution.py:27
  674.3 5.7 collective-permute-done.42
  680.8 2.7 bitcast_convert_fusion
  684.0 3.0 bitcast_convert_fusion.1
  (574 shorter events, 213.3 us)
Async XLA Ops:
  2.9 44.9 %collective-permute-start.6 = (bf16[192,1536]{1,0:T(8,128)(2,1)}, bf16[192,1536]{1,0:T(8,128)(2,1)}, u32[]{:S(2)}, u32[]{:S(2)}) collective-permute-start(bf16[192,1536]{1,0:T(8,128)(2,1)} %constant_dynamic-slice_fusion.2), channel_id=1, source_target_pairs={{0,1},{1,0},{2,3},{3,2},{4,5},{5,4},{6,7},{7,6},{8,9},{9,8},{10,11... | collective-permute-start | bytes 1769480 | tf_op jit(solution)/shard_map/ppermute | solution.py:48
  7.7 38.0 %collective-permute-start = (bf16[576,384]{1,0:T(8,128)(2,1)}, bf16[576,384]{1,0:T(8,128)(2,1)}, u32[]{:S(2)}, u32[]{:S(2)}) collective-permute-start(bf16[576,384]{1,0:T(8,128)(2,1)} %constant_dynamic-slice_fusion.4), channel_id=1, source_target_pairs={{0,1},{1,0},{2,3},{3,2},{4,5},{5,4},{6,7},{7,6},{8,9},{9,8},{10,11... | collective-permute-start | bytes 1327112 | tf_op jit(solution)/shard_map/ppermute | solution.py:48
  8.7 24.2 %collective-permute-start.3 = (bf16[96,768]{1,0:T(8,128)(2,1)S(1)}, bf16[96,768]{1,0:T(8,128)(2,1)S(1)}, u32[]{:S(2)}, u32[]{:S(2)}) collective-permute-start(bf16[96,768]{1,0:T(8,128)(2,1)S(1)} %constant_dynamic-slice_fusion.3), channel_id=1, source_target_pairs={{0,1},{1,0},{2,3},{3,2},{4,5},{5,4},{6,7},{7,6},{8,9},{9,8},{10,11... | collective-permute-start | bytes 442376 | tf_op jit(solution)/shard_map/ppermute | solution.py:48
  12.8 35.1 %collective-permute-start.9 = (bf16[384,768]{1,0:T(8,128)(2,1)}, bf16[384,768]{1,0:T(8,128)(2,1)}, u32[]{:S(2)}, u32[]{:S(2)}) collective-permute-start(bf16[384,768]{1,0:T(8,128)(2,1)} %constant_dynamic-slice_fusion.1), channel_id=1, source_target_pairs={{0,1},{1,0},{2,3},{3,2},{4,5},{5,4},{6,7},{7,6},{8,9},{9,8},{10,11... | collective-permute-start | bytes 1769480 | tf_op jit(solution)/shard_map/ppermute | solution.py:48
  14.3 82.4 %copy-start.108 = (f32[2,256]{1,0:T(2,128)}, f32[2,256]{1,0:T(2,128)S(1)}, u32[]{:S(2)}) copy-start(f32[2,256]{1,0:T(2,128)S(1)} %broadcast_multiply_fusion.11) | copy-start | bytes 6148
  32.8 5.2 collective-permute-start.4
  34.9 61.9 %copy-start.114 = (f32[2,256]{1,0:T(2,128)}, f32[2,256]{1,0:T(2,128)S(1)}, u32[]{:S(2)}) copy-start(f32[2,256]{1,0:T(2,128)S(1)} %add_rsqrt_fusion.3) | copy-start | bytes 6148
  38.1 11.8 %collective-permute-start.5 = (bf16[192,768]{1,0:T(8,128)(2,1)S(1)}, bf16[192,768]{1,0:T(8,128)(2,1)}, u32[]{:S(2)}, u32[]{:S(2)}) collective-permute-start(bf16[192,768]{1,0:T(8,128)(2,1)S(1)} %bitcast.448), channel_id=1, source_target_pairs={{0,2},{2,0},{1,3},{3,1},{4,6},{6,4},{5,7},{7,5},{8,10},{10,8},{9,1... | collective-permute-start | bytes 884744 | tf_op jit(solution)/shard_map/ppermute | solution.py:50
  45.7 13.3 %collective-permute-start.1 = (bf16[576,384]{1,0:T(8,128)(2,1)}, bf16[576,384]{1,0:T(8,128)(2,1)S(1)}, u32[]{:S(2)}, u32[]{:S(2)}) collective-permute-start(bf16[576,384]{1,0:T(8,128)(2,1)} %collective-permute-done), channel_id=1, source_target_pairs={{0,4},{4,0},{1,5},{5,1},{2,6},{6,2},{3,7},{7,3},{8,12},{12,8},{9,1... | collective-permute-start | bytes 1327112 | tf_op jit(solution)/shard_map/ppermute | solution.py:49
  47.7 78.1 %copy-start.98 = (f32[768]{0:T(1024)}, f32[768]{0:T(1024)S(1)}, u32[]{:S(2)}) copy-start(f32[768]{0:T(1024)S(1)} %get-tuple-element.116) | copy-start | bytes 9220
  47.8 78.1 %copy-start.112 = (f32[768]{0:T(1024)}, f32[768]{0:T(1024)S(1)}, u32[]{:S(2)}) copy-start(f32[768]{0:T(1024)S(1)} %get-tuple-element.28) | copy-start | bytes 9220
  47.8 23.8 %collective-permute-start.7 = (bf16[192,1536]{1,0:T(8,128)(2,1)}, bf16[192,1536]{1,0:T(8,128)(2,1)S(1)}, u32[]{:S(2)}, u32[]{:S(2)}) collective-permute-start(bf16[192,1536]{1,0:T(8,128)(2,1)} %collective-permute-done.6), channel_id=1, source_target_pairs={{0,4},{4,0},{1,5},{5,1},{2,6},{6,2},{3,7},{7,3},{8,12},{12,8},{9,1... | collective-permute-start | bytes 1769480 | tf_op jit(solution)/shard_map/ppermute | solution.py:49
  47.9 36.1 %collective-permute-start.10 = (bf16[384,768]{1,0:T(8,128)(2,1)}, bf16[384,768]{1,0:T(8,128)(2,1)S(1)}, u32[]{:S(2)}, u32[]{:S(2)}) collective-permute-start(bf16[384,768]{1,0:T(8,128)(2,1)} %collective-permute-done.9), channel_id=1, source_target_pairs={{0,4},{4,0},{1,5},{5,1},{2,6},{6,2},{3,7},{7,3},{8,12},{12,8},{9,1... | collective-permute-start | bytes 1769480 | tf_op jit(solution)/shard_map/ppermute | solution.py:49
  60.1 26.1 %collective-permute-start.2 = (bf16[1152,384]{1,0:T(8,128)(2,1)S(1)}, bf16[1152,384]{1,0:T(8,128)(2,1)S(1)}, u32[]{:S(2)}, u32[]{:S(2)}) collective-permute-start(bf16[1152,384]{1,0:T(8,128)(2,1)S(1)} %bitcast.412), channel_id=1, source_target_pairs={{0,2},{2,0},{1,3},{3,1},{4,6},{6,4},{5,7},{7,5},{8,10},{10,8},{9,1... | collective-permute-start | bytes 2654216 | tf_op jit(solution)/shard_map/ppermute | solution.py:50
  73.8 37.6 %collective-permute-start.8 = (bf16[384,1536]{1,0:T(8,128)(2,1)}, bf16[384,1536]{1,0:T(8,128)(2,1)}, u32[]{:S(2)}, u32[]{:S(2)}) collective-permute-start(bf16[384,1536]{1,0:T(8,128)(2,1)} %bitcast.30), channel_id=1, source_target_pairs={{0,2},{2,0},{1,3},{3,1},{4,6},{6,4},{5,7},{7,5},{8,10},{10,8},{9,1... | collective-permute-start | bytes 3538952 | tf_op jit(solution)/shard_map/ppermute | solution.py:50
  86.3 27.2 %collective-permute-start.11 = (bf16[768,768]{1,0:T(8,128)(2,1)}, bf16[768,768]{1,0:T(8,128)(2,1)}, u32[]{:S(2)}, u32[]{:S(2)}) collective-permute-start(bf16[768,768]{1,0:T(8,128)(2,1)} %bitcast.37), channel_id=1, source_target_pairs={{0,2},{2,0},{1,3},{3,1},{4,6},{6,4},{5,7},{7,5},{8,10},{10,8},{9,1... | collective-permute-start | bytes 3538952 | tf_op jit(solution)/shard_map/ppermute | solution.py:50
  221.3 85.8 %copy-start.3 = (f32[2,512,768]{2,1,0:T(8,128)}, f32[2,512,768]{2,1,0:T(8,128)S(1)}, u32[]{:S(2)}) copy-start(f32[2,512,768]{2,1,0:T(8,128)S(1)} %multiply_add_fusion) | copy-start | bytes 9437188
  384.1 53.6 %collective-permute-start.54 = (f32[5,768]{1,0:T(8,128)S(1)}, f32[5,768]{1,0:T(8,128)S(1)}, u32[]{:S(2)}, u32[]{:S(2)}) collective-permute-start(f32[5,768]{1,0:T(8,128)S(1)} %stack.339), channel_id=1, source_target_pairs={{0,2},{2,0},{1,3},{3,1},{4,6},{6,4},{5,7},{7,5},{8,10},{10,8},{9,1... | collective-permute-start | bytes 46088 | tf_op jit(solution)/shard_map/ppermute | solution.py:27
  405.1 93.3 %collective-permute-start.45 = (bf16[768,768]{1,0:T(8,128)(2,1)}, bf16[768,768]{1,0:T(8,128)(2,1)}, u32[]{:S(2)}, u32[]{:S(2)}) collective-permute-start(bf16[768,768]{1,0:T(8,128)(2,1)} %dynamic-slice_convert_fusion), channel_id=1, source_target_pairs={{0,2},{2,0},{1,3},{3,1},{4,6},{6,4},{5,7},{7,5},{8,10},{10,8},{9,1... | collective-permute-start | bytes 3538952 | tf_op jit(solution)/shard_map/ppermute | solution.py:58
  408.1 155.1 %collective-permute-start.44 = (bf16[768,768]{1,0:T(8,128)(2,1)}, bf16[768,768]{1,0:T(8,128)(2,1)}, u32[]{:S(2)}, u32[]{:S(2)}) collective-permute-start(bf16[768,768]{1,0:T(8,128)(2,1)} %dynamic-slice_convert_fusion.1), channel_id=1, source_target_pairs={{0,2},{2,0},{1,3},{3,1},{4,6},{6,4},{5,7},{7,5},{8,10},{10,8},{9,1... | collective-permute-start | bytes 3538952 | tf_op jit(solution)/shard_map/ppermute | solution.py:60
  425.6 21.8 %collective-permute-start.25 = (bf16[192,768]{1,0:T(8,128)(2,1)S(1)}, bf16[192,768]{1,0:T(8,128)(2,1)S(1)}, u32[]{:S(2)}, u32[]{:S(2)}) collective-permute-start(bf16[192,768]{1,0:T(8,128)(2,1)S(1)} %dynamic-slice_convert_fusion.11), channel_id=1, source_target_pairs={{0,2},{2,0},{1,3},{3,1},{4,6},{6,4},{5,7},{7,5},{8,10},{10,8},{9,1... | collective-permute-start | bytes 884744 | tf_op jit(solution)/shard_map/ppermute | solution.py:58
  426.2 27.9 %collective-permute-start.24 = (bf16[192,768]{1,0:T(8,128)(2,1)S(1)}, bf16[192,768]{1,0:T(8,128)(2,1)S(1)}, u32[]{:S(2)}, u32[]{:S(2)}) collective-permute-start(bf16[192,768]{1,0:T(8,128)(2,1)S(1)} %dynamic-slice_convert_fusion.12), channel_id=1, source_target_pairs={{0,2},{2,0},{1,3},{3,1},{4,6},{6,4},{5,7},{7,5},{8,10},{10,8},{9,1... | collective-permute-start | bytes 884744 | tf_op jit(solution)/shard_map/ppermute | solution.py:60
  437.8 3.9 collective-permute-start.55
  441.7 3.8 collective-permute-start.56
  445.5 3.9 collective-permute-start.57
  447.5 8.5 %collective-permute-start.26 = (bf16[192,768]{1,0:T(8,128)(2,1)S(1)}, bf16[192,768]{1,0:T(8,128)(2,1)S(1)}, u32[]{:S(2)}, u32[]{:S(2)}) collective-permute-start(bf16[192,768]{1,0:T(8,128)(2,1)S(1)} %add_convert_fusion.8), channel_id=1, source_target_pairs={{0,1},{1,0},{2,3},{3,2},{4,5},{5,4},{6,7},{7,6},{8,9},{9,8},{10,11... | collective-permute-start | bytes 884744 | tf_op jit(solution)/shard_map/ppermute | solution.py:62
  449.4 4.7 collective-permute-start.58
  454.1 42.8 %collective-permute-start.35 = (bf16[384,1536]{1,0:T(8,128)(2,1)S(1)}, bf16[384,1536]{1,0:T(8,128)(2,1)S(1)}, u32[]{:S(2)}, u32[]{:S(2)}) collective-permute-start(bf16[384,1536]{1,0:T(8,128)(2,1)S(1)} %dynamic-slice_convert_fusion.2), channel_id=1, source_target_pairs={{0,2},{2,0},{1,3},{3,1},{4,6},{6,4},{5,7},{7,5},{8,10},{10,8},{9,1... | collective-permute-start | bytes 3538952 | tf_op jit(solution)/shard_map/ppermute | solution.py:58
  454.2 20.1 %collective-permute-start.13 = (bf16[2,256,768]{2,1,0:T(8,128)(2,1)S(1)}, bf16[2,256,768]{2,1,0:T(8,128)(2,1)S(1)}, u32[]{:S(2)}, u32[]{:S(2)}) collective-permute-start(bf16[2,256,768]{2,1,0:T(8,128)(2,1)S(1)} %fusion.37), channel_id=1, source_target_pairs={{0,1},{1,0},{2,3},{3,2},{4,5},{5,4},{6,7},{7,6},{8,9},{9,8},{10,11... | collective-permute-start | bytes 2359304 | tf_op jit(solution)/shard_map/ppermute | solution.py:210
  456.2 6.0 collective-permute-start.27
  462.2 4.4 collective-permute-start.28
  466.7 22.2 %collective-permute-start.15 = (bf16[1152,384]{1,0:T(8,128)(2,1)S(1)}, bf16[1152,384]{1,0:T(8,128)(2,1)S(1)}, u32[]{:S(2)}, u32[]{:S(2)}) collective-permute-start(bf16[1152,384]{1,0:T(8,128)(2,1)S(1)} %dynamic-slice_convert_fusion.4), channel_id=1, source_target_pairs={{0,2},{2,0},{1,3},{3,1},{4,6},{6,4},{5,7},{7,5},{8,10},{10,8},{9,1... | collective-permute-start | bytes 2654216 | tf_op jit(solution)/shard_map/ppermute | solution.py:58
  474.2 5.3 collective-permute-start.29
  479.5 4.9 collective-permute-start.30
  484.4 4.4 collective-permute-start.31
  488.9 98.6 %collective-permute-start.34 = (bf16[384,1536]{1,0:T(8,128)(2,1)}, bf16[384,1536]{1,0:T(8,128)(2,1)}, u32[]{:S(2)}, u32[]{:S(2)}) collective-permute-start(bf16[384,1536]{1,0:T(8,128)(2,1)} %dynamic-slice_convert_fusion.3), channel_id=1, source_target_pairs={{0,2},{2,0},{1,3},{3,1},{4,6},{6,4},{5,7},{7,5},{8,10},{10,8},{9,1... | collective-permute-start | bytes 3538952 | tf_op jit(solution)/shard_map/ppermute | solution.py:60
  488.9 6.3 collective-permute-start.32
  495.3 37.3 %collective-permute-start.12 = (bf16[2,512,768]{2,0,1:T(2,128)(2,1)S(1)}, bf16[2,512,768]{2,0,1:T(2,128)(2,1)S(1)}, u32[]{:S(2)}, u32[]{:S(2)}) collective-permute-start(bf16[2,512,768]{2,0,1:T(2,128)(2,1)S(1)} %bitcast.408), channel_id=1, source_target_pairs={{0,1},{1,0},{2,3},{3,2},{4,5},{5,4},{6,7},{7,6},{8,9},{9,8},{10,11... | collective-permute-start | bytes 4718600 | tf_op jit(solution)/shard_map/ppermute | solution.py:192
  496.9 4.6 collective-permute-start.33
  498.4 39.0 %collective-permute-start.14 = (bf16[1152,384]{1,0:T(8,128)(2,1)S(1)}, bf16[1152,384]{1,0:T(8,128)(2,1)S(1)}, u32[]{:S(2)}, u32[]{:S(2)}) collective-permute-start(bf16[1152,384]{1,0:T(8,128)(2,1)S(1)} %dynamic-slice_convert_fusion.5), channel_id=1, source_target_pairs={{0,2},{2,0},{1,3},{3,1},{4,6},{6,4},{5,7},{7,5},{8,10},{10,8},{9,1... | collective-permute-start | bytes 2654216 | tf_op jit(solution)/shard_map/ppermute | solution.py:60
  501.6 49.9 %collective-permute-start.16 = (bf16[1152,384]{1,0:T(8,128)(2,1)S(1)}, bf16[1152,384]{1,0:T(8,128)(2,1)S(1)}, u32[]{:S(2)}, u32[]{:S(2)}) collective-permute-start(bf16[1152,384]{1,0:T(8,128)(2,1)S(1)} %add_convert_fusion.4), channel_id=1, source_target_pairs={{0,1},{1,0},{2,3},{3,2},{4,5},{5,4},{6,7},{7,6},{8,9},{9,8},{10,11... | collective-permute-start | bytes 2654216 | tf_op jit(solution)/shard_map/ppermute | solution.py:62
  532.6 44.3 %collective-permute-start.46 = (bf16[768,768]{1,0:T(8,128)(2,1)}, bf16[768,768]{1,0:T(8,128)(2,1)}, u32[]{:S(2)}, u32[]{:S(2)}) collective-permute-start(bf16[768,768]{1,0:T(8,128)(2,1)} %add_convert_fusion.2), channel_id=1, source_target_pairs={{0,1},{1,0},{2,3},{3,2},{4,5},{5,4},{6,7},{7,6},{8,9},{9,8},{10,11... | collective-permute-start | bytes 3538952 | tf_op jit(solution)/shard_map/ppermute | solution.py:62
  537.5 63.3 %collective-permute-start.36 = (bf16[384,1536]{1,0:T(8,128)(2,1)}, bf16[384,1536]{1,0:T(8,128)(2,1)S(1)}, u32[]{:S(2)}, u32[]{:S(2)}) collective-permute-start(bf16[384,1536]{1,0:T(8,128)(2,1)} %add_convert_fusion.3), channel_id=1, source_target_pairs={{0,1},{1,0},{2,3},{3,2},{4,5},{5,4},{6,7},{7,6},{8,9},{9,8},{10,11... | collective-permute-start | bytes 3538952 | tf_op jit(solution)/shard_map/ppermute | solution.py:62
  551.9 9.7 %collective-permute-start.17 = (bf16[576,384]{1,0:T(8,128)(2,1)S(1)}, bf16[576,384]{1,0:T(8,128)(2,1)S(1)}, u32[]{:S(2)}, u32[]{:S(2)}) collective-permute-start(bf16[576,384]{1,0:T(8,128)(2,1)S(1)} %dynamic-slice_convert_fusion.8), channel_id=1, source_target_pairs={{0,4},{4,0},{1,5},{5,1},{2,6},{6,2},{3,7},{7,3},{8,12},{12,8},{9,1... | collective-permute-start | bytes 1327112 | tf_op jit(solution)/shard_map/ppermute | solution.py:27
  561.7 17.3 %collective-permute-start.18 = (bf16[288,384]{1,0:T(8,128)(2,1)S(1)}, bf16[288,384]{1,0:T(8,128)(2,1)S(1)}, u32[]{:S(2)}, u32[]{:S(2)}) collective-permute-start(bf16[288,384]{1,0:T(8,128)(2,1)S(1)} %dynamic-slice_convert_fusion.13), channel_id=1, source_target_pairs={{0,8},{8,0},{16,24},{24,16},{1,9},{9,1},{17,25},{25,17},{2,10},{10... | collective-permute-start | bytes 663560 | tf_op jit(solution)/shard_map/ppermute | solution.py:27
  579.1 6.9 %collective-permute-start.19 = (bf16[144,384]{1,0:T(8,128)(2,1)S(1)}, bf16[144,384]{1,0:T(8,128)(2,1)S(1)}, u32[]{:S(2)}, u32[]{:S(2)}) collective-permute-start(bf16[144,384]{1,0:T(8,128)(2,1)S(1)} %dynamic-slice_convert_fusion.17), channel_id=1, source_target_pairs={{0,16},{8,24},{16,0},{24,8},{1,17},{9,25},{17,1},{25,9},{2,18},{10... | collective-permute-start | bytes 331784 | tf_op jit(solution)/shard_map/ppermute | solution.py:27
  581.7 28.9 %collective-permute-start.47 = (bf16[384,768]{1,0:T(8,128)(2,1)S(1)}, bf16[384,768]{1,0:T(8,128)(2,1)S(1)}, u32[]{:S(2)}, u32[]{:S(2)}) collective-permute-start(bf16[384,768]{1,0:T(8,128)(2,1)S(1)} %dynamic-slice_convert_fusion.6), channel_id=1, source_target_pairs={{0,4},{4,0},{1,5},{5,1},{2,6},{6,2},{3,7},{7,3},{8,12},{12,8},{9,1... | collective-permute-start | bytes 1769480 | tf_op jit(solution)/shard_map/ppermute | solution.py:27
  586.0 16.5 %collective-permute-start.20 = (bf16[144,384]{1,0:T(8,128)(2,1)S(1)}, bf16[144,384]{1,0:T(8,128)(2,1)S(1)}, u32[]{:S(2)}, u32[]{:S(2)}) collective-permute-start(bf16[144,384]{1,0:T(8,128)(2,1)S(1)} %add_convert_fusion.11), channel_id=1, source_target_pairs={{0,16},{8,24},{16,0},{24,8},{1,17},{9,25},{17,1},{25,9},{2,18},{10... | collective-permute-start | bytes 331784 | tf_op jit(solution)/shard_map/ppermute | solution.py:27
  602.6 6.2 collective-permute-start.21
  604.1 16.3 %collective-permute-start.37 = (bf16[192,1536]{1,0:T(8,128)(2,1)S(1)}, bf16[192,1536]{1,0:T(8,128)(2,1)S(1)}, u32[]{:S(2)}, u32[]{:S(2)}) collective-permute-start(bf16[192,1536]{1,0:T(8,128)(2,1)S(1)} %dynamic-slice_convert_fusion.7), channel_id=1, source_target_pairs={{0,4},{4,0},{1,5},{5,1},{2,6},{6,2},{3,7},{7,3},{8,12},{12,8},{9,1... | collective-permute-start | bytes 1769480 | tf_op jit(solution)/shard_map/ppermute | solution.py:27
  609.0 22.6 %collective-permute-start.22 = (bf16[576,384]{1,0:T(8,128)(2,1)S(1)}, bf16[576,384]{1,0:T(8,128)(2,1)S(1)}, u32[]{:S(2)}, u32[]{:S(2)}) collective-permute-start(bf16[576,384]{1,0:T(8,128)(2,1)S(1)} %bitcast.446), channel_id=1, source_target_pairs={{0,4},{4,0},{1,5},{5,1},{2,6},{6,2},{3,7},{7,3},{8,12},{12,8},{9,1... | collective-permute-start | bytes 1327112 | tf_op jit(solution)/shard_map/ppermute | solution.py:27
  610.8 10.6 %collective-permute-start.48 = (bf16[192,768]{1,0:T(8,128)(2,1)S(1)}, bf16[192,768]{1,0:T(8,128)(2,1)S(1)}, u32[]{:S(2)}, u32[]{:S(2)}) collective-permute-start(bf16[192,768]{1,0:T(8,128)(2,1)S(1)} %dynamic-slice_convert_fusion.9), channel_id=1, source_target_pairs={{0,8},{8,0},{16,24},{24,16},{1,9},{9,1},{17,25},{25,17},{2,10},{10... | collective-permute-start | bytes 884744 | tf_op jit(solution)/shard_map/ppermute | solution.py:27
  620.7 7.9 %collective-permute-start.38 = (bf16[96,1536]{1,0:T(8,128)(2,1)S(1)}, bf16[96,1536]{1,0:T(8,128)(2,1)S(1)}, u32[]{:S(2)}, u32[]{:S(2)}) collective-permute-start(bf16[96,1536]{1,0:T(8,128)(2,1)S(1)} %dynamic-slice_convert_fusion.10), channel_id=1, source_target_pairs={{0,8},{8,0},{16,24},{24,16},{1,9},{9,1},{17,25},{25,17},{2,10},{10... | collective-permute-start | bytes 884744 | tf_op jit(solution)/shard_map/ppermute | solution.py:27
  621.4 10.4 %collective-permute-start.49 = (bf16[96,768]{1,0:T(8,128)(2,1)S(1)}, bf16[96,768]{1,0:T(8,128)(2,1)S(1)}, u32[]{:S(2)}, u32[]{:S(2)}) collective-permute-start(bf16[96,768]{1,0:T(8,128)(2,1)S(1)} %dynamic-slice_convert_fusion.14), channel_id=1, source_target_pairs={{0,16},{8,24},{16,0},{24,8},{1,17},{9,25},{17,1},{25,9},{2,18},{10... | collective-permute-start | bytes 442376 | tf_op jit(solution)/shard_map/ppermute | solution.py:27
  628.7 12.2 %collective-permute-start.39 = (bf16[48,1536]{1,0:T(8,128)(2,1)S(1)}, bf16[48,1536]{1,0:T(8,128)(2,1)S(1)}, u32[]{:S(2)}, u32[]{:S(2)}) collective-permute-start(bf16[48,1536]{1,0:T(8,128)(2,1)S(1)} %dynamic-slice_convert_fusion.15), channel_id=1, source_target_pairs={{0,16},{8,24},{16,0},{24,8},{1,17},{9,25},{17,1},{25,9},{2,18},{10... | collective-permute-start | bytes 442376 | tf_op jit(solution)/shard_map/ppermute | solution.py:27
  631.8 40.0 %collective-permute-start.23 = (bf16[1152,384]{1,0:T(8,128)(2,1)S(1)}, bf16[1152,384]{1,0:T(8,128)(2,1)S(1)}, u32[]{:S(2)}, u32[]{:S(2)}) collective-permute-start(bf16[1152,384]{1,0:T(8,128)(2,1)S(1)} %bitcast.411), channel_id=1, source_target_pairs={{0,2},{2,0},{1,3},{3,1},{4,6},{6,4},{5,7},{7,5},{8,10},{10,8},{9,1... | collective-permute-start | bytes 2654216 | tf_op jit(solution)/shard_map/ppermute | solution.py:72
  631.9 12.1 %collective-permute-start.50 = (bf16[96,768]{1,0:T(8,128)(2,1)S(1)}, bf16[96,768]{1,0:T(8,128)(2,1)S(1)}, u32[]{:S(2)}, u32[]{:S(2)}) collective-permute-start(bf16[96,768]{1,0:T(8,128)(2,1)S(1)} %add_convert_fusion.9), channel_id=1, source_target_pairs={{0,16},{8,24},{16,0},{24,8},{1,17},{9,25},{17,1},{25,9},{2,18},{10... | collective-permute-start | bytes 442376 | tf_op jit(solution)/shard_map/ppermute | solution.py:27
  640.9 6.6 collective-permute-start.40
  644.1 10.9 %collective-permute-start.51 = (bf16[192,768]{1,0:T(8,128)(2,1)S(1)}, bf16[192,768]{1,0:T(8,128)(2,1)S(1)}, u32[]{:S(2)}, u32[]{:S(2)}) collective-permute-start(bf16[192,768]{1,0:T(8,128)(2,1)S(1)} %bitcast.450), channel_id=1, source_target_pairs={{0,8},{8,0},{16,24},{24,16},{1,9},{9,1},{17,25},{25,17},{2,10},{10... | collective-permute-start | bytes 884744 | tf_op jit(solution)/shard_map/ppermute | solution.py:27
  647.6 12.2 %collective-permute-start.41 = (bf16[96,1536]{1,0:T(8,128)(2,1)S(1)}, bf16[96,1536]{1,0:T(8,128)(2,1)S(1)}, u32[]{:S(2)}, u32[]{:S(2)}) collective-permute-start(bf16[96,1536]{1,0:T(8,128)(2,1)S(1)} %bitcast.451), channel_id=1, source_target_pairs={{0,8},{8,0},{16,24},{24,16},{1,9},{9,1},{17,25},{25,17},{2,10},{10... | collective-permute-start | bytes 884744 | tf_op jit(solution)/shard_map/ppermute | solution.py:27
  655.1 16.3 %collective-permute-start.52 = (bf16[384,768]{1,0:T(8,128)(2,1)S(1)}, bf16[384,768]{1,0:T(8,128)(2,1)S(1)}, u32[]{:S(2)}, u32[]{:S(2)}) collective-permute-start(bf16[384,768]{1,0:T(8,128)(2,1)S(1)} %bitcast.437), channel_id=1, source_target_pairs={{0,4},{4,0},{1,5},{5,1},{2,6},{6,2},{3,7},{7,3},{8,12},{12,8},{9,1... | collective-permute-start | bytes 1769480 | tf_op jit(solution)/shard_map/ppermute | solution.py:27
  659.9 20.1 %collective-permute-start.42 = (bf16[192,1536]{1,0:T(8,128)(2,1)S(1)}, bf16[192,1536]{1,0:T(8,128)(2,1)S(1)}, u32[]{:S(2)}, u32[]{:S(2)}) collective-permute-start(bf16[192,1536]{1,0:T(8,128)(2,1)S(1)} %bitcast.436), channel_id=1, source_target_pairs={{0,4},{4,0},{1,5},{5,1},{2,6},{6,2},{3,7},{7,3},{8,12},{12,8},{9,1... | collective-permute-start | bytes 1769480 | tf_op jit(solution)/shard_map/ppermute | solution.py:27
  671.7 8.6 %collective-permute-start.53 = (bf16[768,768]{1,0:T(8,128)(2,1)S(1)}, bf16[768,768]{1,0:T(8,128)(2,1)S(1)}, u32[]{:S(2)}, u32[]{:S(2)}) collective-permute-start(bf16[768,768]{1,0:T(8,128)(2,1)S(1)} %bitcast.409), channel_id=1, source_target_pairs={{0,2},{2,0},{1,3},{3,1},{4,6},{6,4},{5,7},{7,5},{8,10},{10,8},{9,1... | collective-permute-start | bytes 3538952 | tf_op jit(solution)/shard_map/ppermute | solution.py:72
  680.2 3.3 collective-permute-start.43
  (131 other events, 833.0 us)
